TPU v7x, 32 devices: a whole 2x2x4 slice. The times are simulated.
32 devices in a mesh: grp: 2 (over x), dev: 16 (over z, y, core).
Axes of the slice: x: 2, y: 2, z: 4, core: 2. Of those that a mesh axis runs over, the one named last changes fastest.
Arguments:
- frames: bfloat16 [80, 64, 1408], P('dev'), may hold values from -100 to 100
- trained: int32 [80], replicated, may hold values from 0 to 3071, as said below
- frame_of: int32 [6144], P('dev'), may hold values from 0 to 3071, as said below
- token_cache: bfloat16 [6144, 1408], P('dev'), may hold values from -100 to 100
- norm_gains: float32 [2, 1408], P('grp'), may hold values from 0.1 to 1.9
- proj_weights: bfloat16 [2, 1408, 4224], P('grp'), may hold values from -4 to 4
- out_weights: bfloat16 [2, 1408, 1408], P('grp'), may hold values from -0.15625 to 0.15625
- patch_cotangent: bfloat16 [80, 64, 1408], P('dev'), may hold values from -0.119628906 to 0.119628906
- time_cotangent: bfloat16 [6144, 1408], P('dev'), may hold values from -6 to 6
Outputs:
- weight_grad: float32 [2, 1408, 1408], P('grp', 'dev')
Inputs may be any that keep to these rules, and one draw needn't show every extreme that they name: `trained`: 80 different frames of the video; among them, for every k, the frames k * 192 and (k + 1) * 192 - 1. `frame_of`: never falls along the tokens; tokens 4 m to 4 m + 3 belong to frames 2 m and 2 m + 1, each frame having 1 to 3 tokens.
All inputs are finite; a program needn't handle non-finite values.
Results may differ from a plain program's by a relative error of at most 0.0078.
Values may be sent and summed in bfloat16 or wider, within the bound.
A program may use at most 192 MiB of HBM per device.

v0:
```python
import jax
import jax.numpy as jnp
from jax import lax
from jax.sharding import PartitionSpec as P

HEADS = 16
HEAD_DIM = 88
SPAN = 128
EPS = 1e-06
HIGH_PRECISION = lax.Precision.HIGHEST


def from_behind(value, axis, steps):
    count = lax.axis_size(axis)
    initial, last = (max(0, -steps), min(count, count - steps))
    return lax.ppermute(value, axis, [(source, source + steps) for source in range(initial, last)])


def with_halo(array, sides, width):
    for axis, dim in sides:
        size, length = (lax.axis_size(axis), array.shape[dim])
        up = [(i, (i + 1) % size) for i in range(size - 1)]
        down = [(j, i) for i, j in up]
        last = lax.slice_in_dim(array, length - width, length, axis=dim)
        initial = lax.slice_in_dim(array, 0, width, axis=dim)
        before = lax.ppermute(last, axis, up)
        after = lax.ppermute(initial, axis, down)
        array = jnp.concatenate([before, array, after], axis=dim)
    return array


def normalize(rows):
    inverse = lax.rsqrt(jnp.mean(rows * rows, axis=-1, keepdims=True) + EPS)
    return (rows * inverse, inverse)


def when_true(flag, compute):

    def skipped():
        return jax.tree.map(jnp.zeros_like, compute())

    return lax.cond(flag, compute, skipped)


def contract_rows(left, right):
    return lax.dot_general(
        left, right, (((0,), (0,)), ((), ())), preferred_element_type=jnp.float32
    )


def contract_exact(left, right):
    return lax.dot_general(left, right, (((0,), (0,)), ((), ())), precision=HIGH_PRECISION)


def contract_cols(left, right):
    return lax.dot_general(
        left, right, (((1,), (1,)), ((), ())), preferred_element_type=jnp.float32
    )


def stack_windows(extended, count):
    return jnp.stack([extended[block * SPAN : (block + 3) * SPAN] for block in range(count)])


def shards(
    frames,
    trained,
    frame_of,
    token_cache,
    norm_gains,
    proj_weights,
    out_weights,
    patch_cotangent,
    time_cotangent,
):
    spatial = lax.axis_index("grp") == 0
    temporal = jnp.logical_not(spatial)
    norm_gain = norm_gains[0]
    in_proj = proj_weights[0]
    out_proj = out_weights[0]
    width = in_proj.shape[0]
    frame_count, patches, _ = frames.shape
    token_count = token_cache.shape[0]
    nblocks = token_count // SPAN
    score_scale = HEAD_DIM ** (-0.5)
    first_token = lax.axis_index("dev") * token_count
    token_total = lax.axis_size("dev") * token_count
    win_pos = (
        first_token
        + (jnp.arange(nblocks, dtype=jnp.int32)[:, None] - 1) * SPAN
        + jnp.arange(3 * SPAN, dtype=jnp.int32)[None, :]
    )
    win_valid = (win_pos >= 0) & (win_pos < token_total)

    def spatial_forward():
        rows = frames.reshape(frame_count * patches, width).astype(jnp.float32)
        scaled_rows, _ = normalize(rows)
        normed = (scaled_rows * norm_gain).astype(jnp.bfloat16)
        packed = jnp.dot(normed, in_proj, preferred_element_type=jnp.float32).astype(jnp.bfloat16)
        packed = packed.reshape(frame_count, patches, 3, HEADS, HEAD_DIM)
        attention_logits = (
            jnp.einsum(
                "fphd,fqhd->fhpq",
                packed[:, :, 0],
                packed[:, :, 1],
                preferred_element_type=jnp.float32,
            )
            * score_scale
        )
        attention_probs = jax.nn.softmax(attention_logits, axis=-1).astype(jnp.bfloat16)
        attended_output = jnp.einsum(
            "fhpq,fqhd->fphd", attention_probs, packed[:, :, 2], preferred_element_type=jnp.float32
        )
        attended_output = attended_output.astype(jnp.bfloat16).reshape(frame_count * patches, width)
        output = rows + jnp.dot(attended_output, out_proj, preferred_element_type=jnp.float32)
        pooled = jnp.mean(output.reshape(frame_count, patches, width), axis=1).astype(jnp.bfloat16)
        return (pooled, attended_output)

    pooled, spatial_mixed = when_true(spatial, spatial_forward)
    handed = from_behind(pooled, "grp", 1)
    arrived = lax.all_gather(handed, "dev", axis=0, tiled=True)

    def temporal_front():
        selector = (frame_of[:, None] == trained[None, :]).astype(jnp.bfloat16)
        inputs = token_cache.astype(jnp.float32) + jnp.dot(
            selector, arrived, preferred_element_type=jnp.float32
        )
        scaled_rows, inverse = normalize(inputs)
        normed = (scaled_rows * norm_gain).astype(jnp.bfloat16)
        packed = jnp.dot(normed, in_proj, preferred_element_type=jnp.float32).astype(jnp.bfloat16)
        return (selector, scaled_rows, inverse, packed[:, :width], packed[:, width:])

    selector, scaled_rows, inverse, queries, key_value = when_true(temporal, temporal_front)
    extended = with_halo(key_value, (("dev", 0),), SPAN)
    key_window = stack_windows(extended, nblocks)
    key_heads = key_window[..., :width].reshape(nblocks, 3 * SPAN, HEADS, HEAD_DIM)
    value_heads = key_window[..., width:].reshape(nblocks, 3 * SPAN, HEADS, HEAD_DIM)
    query_heads = queries.reshape(nblocks, SPAN, HEADS, HEAD_DIM)

    def temporal_attend():
        attention_logits = (
            jnp.einsum(
                "bqhd,bkhd->bhqk", query_heads, key_heads, preferred_element_type=jnp.float32
            )
            * score_scale
        )
        attention_logits = jnp.where(win_valid[:, None, None, :], attention_logits, -1e30)
        row_top = jnp.max(attention_logits, axis=-1, keepdims=True)
        log_total = row_top + jnp.log(
            jnp.sum(jnp.exp(attention_logits - row_top), axis=-1, keepdims=True)
        )
        chances = jnp.exp(attention_logits - log_total)
        chance_weights = chances.astype(jnp.bfloat16)
        attended_output = jnp.einsum(
            "bhqk,bkhd->bqhd", chance_weights, value_heads, preferred_element_type=jnp.float32
        )
        return (
            chances,
            chance_weights,
            log_total[..., 0],
            attended_output.astype(jnp.bfloat16).reshape(token_count, width),
        )

    chances, chance_weights, log_total, time_mixed = when_true(temporal, temporal_attend)

    def temporal_grads():
        grad_mixed = contract_cols(time_cotangent, out_proj).astype(jnp.bfloat16)
        grad_heads = grad_mixed.reshape(nblocks, SPAN, HEADS, HEAD_DIM)
        mixed_heads = time_mixed.reshape(nblocks, SPAN, HEADS, HEAD_DIM)
        row_delta = jnp.sum(
            grad_heads.astype(jnp.float32) * mixed_heads.astype(jnp.float32), axis=-1
        ).transpose(0, 2, 1)
        probability_gradient = jnp.einsum(
            "bqhd,bkhd->bhqk", grad_heads, value_heads, preferred_element_type=jnp.float32
        )
        logit_gradient = (chances * (probability_gradient - row_delta[..., None])).astype(
            jnp.bfloat16
        )
        query_gradient = (
            jnp.einsum(
                "bhqk,bkhd->bqhd", logit_gradient, key_heads, preferred_element_type=jnp.float32
            )
            * score_scale
        )
        return (grad_mixed, row_delta, logit_gradient, query_gradient.reshape(token_count, width))

    grad_mixed, row_delta, logit_gradient, query_gradient = when_true(temporal, temporal_grads)
    stats = jnp.concatenate(
        [
            log_total.transpose(0, 2, 1).reshape(token_count, HEADS),
            row_delta.transpose(0, 2, 1).reshape(token_count, HEADS),
        ],
        axis=-1,
    )
    near_stats = with_halo(stats, (("dev", 0),), SPAN)
    near_rows = with_halo(jnp.concatenate([queries, grad_mixed], axis=-1), (("dev", 0),), SPAN)

    def rim_keys():
        row_window = stack_windows(near_rows, nblocks)
        stat_window = stack_windows(near_stats, nblocks)
        query_part = row_window[..., :width].reshape(nblocks, 3 * SPAN, HEADS, HEAD_DIM)
        grad_part = row_window[..., width:].reshape(nblocks, 3 * SPAN, HEADS, HEAD_DIM)
        totals = stat_window[..., :HEADS].transpose(0, 2, 1)
        deltas = stat_window[..., HEADS:].transpose(0, 2, 1)
        own_keys = key_value[:, :width].reshape(nblocks, SPAN, HEADS, HEAD_DIM)
        own_values = key_value[:, width:].reshape(nblocks, SPAN, HEADS, HEAD_DIM)
        attention_logits = (
            jnp.einsum("bqhd,bkhd->bhqk", query_part, own_keys, preferred_element_type=jnp.float32)
            * score_scale
        )
        again = jnp.where(
            win_valid[:, None, :, None],
            jnp.exp(
                jnp.where(win_valid[:, None, :, None], attention_logits - totals[..., None], 0.0)
            ),
            0.0,
        )
        probability_gradient = jnp.einsum(
            "bqhd,bkhd->bhqk", grad_part, own_values, preferred_element_type=jnp.float32
        )
        part_score = (again * (probability_gradient - deltas[..., None])).astype(jnp.bfloat16)
        key_gradient = (
            jnp.einsum(
                "bhqk,bqhd->bkhd", part_score, query_part, preferred_element_type=jnp.float32
            )
            * score_scale
        )
        value_gradient = jnp.einsum(
            "bhqk,bqhd->bkhd",
            again.astype(jnp.bfloat16),
            grad_part,
            preferred_element_type=jnp.float32,
        )
        return jnp.concatenate(
            [key_gradient.reshape(token_count, width), value_gradient.reshape(token_count, width)],
            axis=-1,
        )

    key_grads = when_true(temporal, rim_keys)

    def temporal_back():
        grad_packed = jnp.concatenate([query_gradient, key_grads], axis=-1).astype(jnp.bfloat16)
        grad_scaled = contract_cols(grad_packed, in_proj) * norm_gain
        grad_inputs = inverse * (
            grad_scaled - scaled_rows * jnp.mean(grad_scaled * scaled_rows, axis=-1, keepdims=True)
        ) + time_cotangent.astype(jnp.float32)
        return contract_exact(selector.astype(jnp.float32), grad_inputs)

    frame_grads = when_true(temporal, temporal_back)
    reduced = lax.psum_scatter(frame_grads, "dev", scatter_dimension=0, tiled=True)
    returned = from_behind(reduced, "grp", -1)

    def spatial_right():
        grads = patch_cotangent.astype(jnp.float32) + returned[:, None, :] / patches
        return grads.reshape(frame_count * patches, width)

    right_side = when_true(spatial, spatial_right)

    def from_frames():
        return contract_exact(spatial_mixed.astype(jnp.float32), right_side)

    def from_tokens():
        return contract_rows(time_mixed, time_cotangent)

    weight_part = lax.psum_scatter(
        lax.cond(spatial, from_frames, from_tokens), "dev", scatter_dimension=0, tiled=True
    )
    return weight_part[None]


def solution(mesh):
    in_specs = (
        P("dev", None, None),
        P(),
        P("dev"),
        P("dev", None),
        P("grp", None),
        P("grp", None, None),
        P("grp", None, None),
        P("dev", None, None),
        P("dev", None),
    )
    out_specs = P("grp", "dev", None)
    return jax.shard_map(shards, mesh=mesh, in_specs=in_specs, out_specs=out_specs, check_vma=False)
```

profile of v0, /device:TPU:0, one launch (start us, length us, event | category | flops | bytes accessed | tf_op | source)
XLA Modules:
  0.0 491.3 jit_solution(10621586428022382250)
XLA Ops:
  6.5 40.0 %conditional.8 = (bf16[5,1408]{1,0:T(8,128)(2,1)S(1)}, bf16[320,1408]{1,0:T(8,128)(2,1)}) conditional(s32[]{:T(128)} %convert_element_type.90, () %tuple.65, (bf16[5,64,1408]{2,1,0:T(8,128)(2,1)}, f32[1,1408]{1,0:T(1,128)}, bf16[1408,4224]{1,0:T(8,128)(2,1)}, bf16[1408,1408]{1,0:T(8,128)(2,1)}) %tuple.143), branch_computations={%region_0.0_spmd, %region_1.0_spmd} | conditional | flops 5198732288 | bytes 54580020 | solution.py:42
  10.3 9.1 %convolution_convert_fusion.1 = bf16[320,4224]{1,0:T(8,128)(2,1)S(1)} fusion(bf16[320,1408]{1,0:T(8,128)(2,1)S(1)} %fusion.44, bf16[1408,4224]{1,0:T(8,128)(2,1)} %get-tuple-element.100), kind=kOutput, calls=%fused_computation.55 | convolution fusion | flops 3807682560 | bytes 15499264 | tf_op jit(solution)/shard_map/cond/branch_1_fun/dot_general | solution.py:99
  19.4 8.5 %reshape.116 = bf16[5,64,3,16,88]{4,3,2,1,0:T(8,128)(2,1)} reshape(bf16[320,4224]{1,0:T(8,128)(2,1)S(1)} %convolution_convert_fusion.1) | data formatting | bytes 5406720 | tf_op jit(solution)/shard_map/cond/branch_1_fun/reshape | solution.py:100
  27.9 3.0 fusion.76
  31.8 3.9 fusion.77
  39.6 5.3 %convolution_add_fusion = f32[320,1408]{1,0:T(8,128)} fusion(bf16[320,1408]{1,0:T(8,128)(2,1)} %reshape.117, bf16[1408,1408]{1,0:T(8,128)(2,1)} %get-tuple-element.101, bf16[320,1408]{1,0:T(8,128)(2,1)S(1)} %bitcast.144), kind=kOutput, calls=%fused_computation.56 | convolution fusion | flops 1269678080 | bytes 7569408 | tf_op jit(solution)/shard_map/cond/branch_1_fun/dot_general | solution.py:115
  49.3 24.1 %all-gather = bf16[16,5,1408]{2,1,0:T(8,128)(2,1)S(1)} all-gather(bf16[1,5,1408]{2,1,0:T(8,128)(2,1)S(1)} %bitcast.152), channel_id=1, replica_groups=mesh['grp'=2,'dev'=16] {'dev'}, dimensions={0}, use_global_device_ids=true | all-gather | bytes 239360 | tf_op jit(solution)/shard_map/all_gather | solution.py:121
  73.5 4.5 conditional.9
  79.4 2.9 copy.69
  83.3 3.1 collective-permute-start.1
  87.7 2.3 constant_dynamic-update-slice_fusion.1
  96.0 6.1 %conditional.10 = (f32[3,16,128,384]{3,2,1,0:T(8,128)}, f32[3,16,128]{2,1,0:T(8,128)S(1)}, bf16[384,1408]{0,1:T(8,128)(2,1)}) conditional(s32[]{:T(128)} %convert_element_type.91, () %tuple.63, (pred[3,384]{1,0:T(4,128)(4,1)S(1)}, bf16[3,128,16,88]{1,0,3,2:T(4,128)(2,1)}, bf16[3,384,16,88]{1,3,2,0:T(8,128)(2,1)S(1)}, ...), branch_computations={%region_9.0_spmd, %region_10.13_spmd} | conditional | flops 856958976 | bytes 60534224 | solution.py:42
  96.0 4.8 broadcast.154
  102.1 6.0 %conditional.11 = (f32[3,16,128]{2,0,1:T(4,128)S(1)}, bf16[384,1408]{0,1:T(8,128)(2,1)}, bf16[384,1408]{0,1:T(8,128)(2,1)}) conditional(s32[]{:T(128)} %convert_element_type.91, () %tuple.72, (bf16[384,1408]{1,0:T(8,128)(2,1)}, bf16[1408,1408]{1,0:T(8,128)(2,1)}, bf16[384,1408]{0,1:T(8,128)(2,1)}, bf16[3,384,16,88]{1,3,2,0:T(8,128)(2,1)}, ...), branch_computations={%region_13.14_spmd, %region_14.16_spmd} | conditional | flops 2363320320 | bytes 39649360 | solution.py:42
  108.0 2.3 constant_dynamic-update-slice_fusion
  111.9 13.2 %collective-permute-start.3 = (bf16[128,2816]{0,1:T(8,128)(2,1)S(1)}, bf16[128,2816]{0,1:T(8,128)(2,1)S(1)}, u32[]{:S(2)}, u32[]{:S(2)}) collective-permute-start(bf16[128,2816]{0,1:T(8,128)(2,1)S(1)} %get-tuple-element.261), channel_id=1, source_target_pairs={{0,1},{1,2},{2,3},{3,4},{4,5},{5,6},{6,7},{7,8},{8,9},{9,10},{10,1... | collective-permute-start | bytes 2162696 | tf_op jit(solution)/shard_map/ppermute | solution.py:26
  126.5 5.0 %collective-permute-start.5 = (f32[128,32]{0,1:T(8,128)S(1)}, f32[128,32]{0,1:T(8,128)S(1)}, u32[]{:S(2)}, u32[]{:S(2)}) collective-permute-start(f32[128,32]{0,1:T(8,128)S(1)} %get-tuple-element.267), channel_id=1, source_target_pairs={{0,1},{1,2},{2,3},{3,4},{4,5},{5,6},{6,7},{7,8},{8,9},{9,10},{10,1... | collective-permute-start | bytes 49160 | tf_op jit(solution)/shard_map/ppermute | solution.py:26
  132.7 3.0 collective-permute-done.6
  139.0 8.4 %conditional.13 = (f32[80,1408]{1,0:T(8,128)}) conditional(s32[]{:T(128)} %convert_element_type.91, () %tuple.71, (f32[384,1]{0,1:T(1,128)S(1)}, bf16[384,1408]{0,1:T(8,128)(2,1)}, bf16[384,2816]{0,1:T(8,128)(2,1)S(1)}, bf16[1408,4224]{1,0:T(8,128)(2,1)}, f32[1,1408]{1,0:T(1,128)}, /*index=5*/f32[384,1408]{1,0:T(8,128)}, ...), branch_computations={%region_18.19_spmd, %region_19.21_spmd} | conditional | flops 5097455616 | bytes 36246600 | solution.py:42
  148.7 213.6 %all-reduce.4.cloned.1.call-done = f32[80,1408]{1,0:T(8,128)} async-done(((f32[80,1408]{1,0:T(8,128)}), f32[80,1408]{1,0:T(8,128)}) %all-reduce.4.cloned.1.call-update) | async-done | bytes 450576
  364.5 4.7 collective-permute-done.7
  370.6 10.3 %conditional.15 = (f32[1408,1408]{1,0:T(8,128)}) conditional(s32[]{:T(128)} %convert_element_type.90, (bf16[384,1408]{0,1:T(8,128)(2,1)}, bf16[384,1408]{1,0:T(8,128)(2,1)S(1)}) %tuple.137, (bf16[320,1408]{1,0:T(8,128)(2,1)}, f32[320,1408]{1,0:T(8,128)S(1)}) %tuple.78), branch_computations={%region_24.25_spmd, %region_25.26_spmd} | conditional | flops 7612661760 | bytes 10633224 | solution.py:266
  370.6 10.3 %fusion.83 = f32[1408,1408]{1,0:T(8,128)} fusion(bf16[320,1408]{1,0:T(8,128)(2,1)} %get-tuple-element.136, f32[320,1408]{1,0:T(8,128)S(1)} %get-tuple-element.137), kind=kOutput, calls=%fused_computation.129 | convolution fusion | flops 7612661760 | bytes 10633216 | tf_op jit(solution)/shard_map/cond/branch_1_fun/dot_general | solution.py:52
  381.0 103.3 %reduce-scatter.4.cloned.1.call-done = f32[88,1408]{1,0:T(8,128)} async-done(((f32[1408,1408]{1,0:T(8,128)}), f32[88,1408]{1,0:T(8,128)}) %reduce-scatter.4.cloned.1.call-update) | async-done | bytes 495632
  (76 shorter events, 44.1 us)
Async XLA Ops:
  6.5 355.7 %all-reduce.4.cloned.1.call-start = ((), (), s32[]{:S(2)}) async-start(), calls=%async_computation.1 | async-start | bytes 901120
  6.5 67.0 %copy-start.15 = (s32[384]{0:T(512)S(1)}, s32[384]{0:T(512)}, u32[]{:S(2)}) copy-start(s32[384]{0:T(512)} %param.27) | copy-start | bytes 4612
  6.5 67.0 %copy-start.16 = (s32[80]{0:T(128)S(1)}, s32[80]{0:T(128)}, u32[]{:S(2)}) copy-start(s32[80]{0:T(128)} %param.26) | copy-start | bytes 964
  36.5 3.1 copy-start.7
  46.5 2.8 collective-permute-start
  78.0 1.3 copy-start.2
  83.3 6.8 %collective-permute-start.1 = (bf16[128,2816]{0,1:T(8,128)(2,1)}, bf16[128,2816]{0,1:T(8,128)(2,1)}, u32[]{:S(2)}, u32[]{:S(2)}) collective-permute-start(bf16[128,2816]{0,1:T(8,128)(2,1)} %get-tuple-element.265), channel_id=1, source_target_pairs={{0,1},{1,2},{2,3},{3,4},{4,5},{5,6},{6,7},{7,8},{8,9},{9,10},{10,1... | collective-permute-start | bytes 2162696 | tf_op jit(solution)/shard_map/ppermute | solution.py:26
  86.4 4.2 collective-permute-start.2
  94.3 1.7 copy-start
  110.4 25.4 %copy-start.1 = (bf16[384,2816]{0,1:T(8,128)(2,1)S(1)}, bf16[384,2816]{0,1:T(8,128)(2,1)}, u32[]{:S(2)}) copy-start(bf16[384,2816]{0,1:T(8,128)(2,1)} %constant_dynamic-update-slice_fusion) | copy-start | bytes 6488068
  111.9 23.8 %collective-permute-start.3 = (bf16[128,2816]{0,1:T(8,128)(2,1)S(1)}, bf16[128,2816]{0,1:T(8,128)(2,1)S(1)}, u32[]{:S(2)}, u32[]{:S(2)}) collective-permute-start(bf16[128,2816]{0,1:T(8,128)(2,1)S(1)} %get-tuple-element.261), channel_id=1, source_target_pairs={{0,1},{1,2},{2,3},{3,4},{4,5},{5,6},{6,7},{7,8},{8,9},{9,10},{10,1... | collective-permute-start | bytes 2162696 | tf_op jit(solution)/shard_map/ppermute | solution.py:26
  125.1 10.7 %collective-permute-start.4 = (bf16[128,2816]{0,1:T(8,128)(2,1)S(1)}, bf16[128,2816]{0,1:T(8,128)(2,1)S(1)}, u32[]{:S(2)}, u32[]{:S(2)}) collective-permute-start(bf16[128,2816]{0,1:T(8,128)(2,1)S(1)} %get-tuple-element.262), channel_id=1, source_target_pairs={{1,0},{2,1},{3,2},{4,3},{5,4},{6,5},{7,6},{8,7},{9,8},{10,9},{11,1... | collective-permute-start | bytes 2162696 | tf_op jit(solution)/shard_map/ppermute | solution.py:27
  126.5 6.3 %collective-permute-start.5 = (f32[128,32]{0,1:T(8,128)S(1)}, f32[128,32]{0,1:T(8,128)S(1)}, u32[]{:S(2)}, u32[]{:S(2)}) collective-permute-start(f32[128,32]{0,1:T(8,128)S(1)} %get-tuple-element.267), channel_id=1, source_target_pairs={{0,1},{1,2},{2,3},{3,4},{4,5},{5,6},{6,7},{7,8},{8,9},{9,10},{10,1... | collective-permute-start | bytes 49160 | tf_op jit(solution)/shard_map/ppermute | solution.py:26
  131.4 4.3 collective-permute-start.6
  135.8 2.6 copy-start.3
  139.0 8.5 %copy-start.17 = (u32[32]{0:T(128)S(1)}, u32[32]{0:T(128)}, u32[]{:S(2)}) copy-start(u32[32]{0:T(128)} %constant.101) | copy-start | bytes 388
  147.5 336.8 %reduce-scatter.4.cloned.1.call-start = ((), (), s32[]{:S(2)}) async-start(), calls=%async_computation.2 | async-start | bytes 8425472
  363.2 6.0 %collective-permute-start.7 = (f32[5,1408]{1,0:T(8,128)S(1)}, f32[5,1408]{1,0:T(8,128)S(1)}, u32[]{:S(2)}, u32[]{:S(2)}) collective-permute-start(f32[5,1408]{1,0:T(8,128)S(1)} %constant_dynamic-slice_fusion), channel_id=1, source_target_pairs={{16,0},{17,1},{18,2},{19,3},{20,4},{21,5},{22,6},{23,7},{24,8},{25... | collective-permute-start | bytes 84488 | tf_op jit(solution)/shard_map/ppermute | solution.py:16
  369.1 1.5 copy-start.5
Sparse Core Ops, SparseCore 0:
  147.6 214.6 all-reduce.3
  381.1 103.1 reduce-scatter.3
where the time goes:
time: 500 us; the launch traced here: 491 us
  waiting for transfers between devices  327 us (65%)
  local copies, waits for them, and re-layouts  44.1 us (9%)
  starting transfers between devices  27.7 us (6%)
  matrix products  26.3 us (5%)
  blocking collectives  24.1 us (5%)
  other arithmetic  15.8 us (3%)
  between operations  14.4 us (3%)
  loops' own time  12.3 us (2%)
    unnamed x4, waiting for transfers between devices  317 us
    all_gather x1, blocking collectives, shards(): arrived = lax.all_gather(handed, 'dev', axis=0, tiled=True)  24.1 us
    ppermute x3, starting transfers between devices, with_halo(): before = lax.ppermute(last, axis, up)  21.2 us
    another operation x7, loops' own time, when_true(): return lax.cond(flag, compute, skipped)  12.3 us
    another operation x13, local copies, waits for them, and re-layouts  11.9 us
    dot_general x1, matrix products, contract_exact(): lax.dot_general(left, right, (((0,), (0,)), ((), ())), precision=HIGH_PRE...  10.3 us
  transfers between devices with their start and end apart: 10, of which 6 were waited for; matrix products, arithmetic and copies ran while one was open for 1% of the time, Pallas kernels for 0%

commit v1 on v0

--- a/solution.py
+++ b/solution.py
@@ -118,7 +118,36 @@
 
     pooled, spatial_mixed = when_true(spatial, spatial_forward)
     handed = from_behind(pooled, "grp", 1)
-    arrived = lax.all_gather(handed, "dev", axis=0, tiled=True)
+    rack = []
+    b_next, o_now, a_next = (lax.axis_size("dev"), lax.axis_index("dev"), handed.shape[0])
+    for s, m in enumerate(handed.shape):
+        rack.append(m * b_next if s == 0 else m)
+    arrived = lax.dynamic_update_slice_in_dim(
+        jnp.zeros(rack, handed.dtype), handed, o_now * a_next, axis=0
+    )
+    jj = 1
+    x_new = row_out = handed
+    while jj < b_next // 2 + 1:
+        steps_seen = []
+        s = 0
+        while s < b_next:
+            steps_seen.append((s, (s + 1) % b_next))
+            s += 1
+        x_new = lax.ppermute(x_new, "dev", steps_seen)
+        arrived = lax.dynamic_update_slice_in_dim(
+            arrived, x_new, (o_now - jj) % b_next * a_next, axis=0
+        )
+        if 2 * jj < b_next:
+            copies = []
+            s = 0
+            while s < b_next:
+                copies.append((s, (s - 1) % b_next))
+                s = s + 1
+            row_out = lax.ppermute(row_out, "dev", copies)
+            arrived = lax.dynamic_update_slice_in_dim(
+                arrived, row_out, (o_now + jj) % b_next * a_next, axis=0
+            )
+        jj = jj + 1
 
     def temporal_front():
         selector = (frame_of[:, None] == trained[None, :]).astype(jnp.bfloat16)

time: 500 us -> 519 us (1.038)
  blocking collectives: 24.1 us -> 0 us
  starting transfers between devices: 27.7 us -> 51.5 us
  waiting for transfers between devices: 327 us -> 345 us
    ppermute x0 -> x15, starting transfers between devices: none -> 31.5 us  [the longest x7 31.4 us: shards(): row_out = lax.ppermute(row_out, 'dev', copies)]
    all_gather x1 -> x0, blocking collectives: 24.1 us -> none  [shards(): arrived = lax.all_gather(handed, 'dev', axis=0, tiled=True)]
    ppermute x0 -> x15, waiting for transfers between devices: none -> 16.4 us  [the longest x8 16.3 us: shards(): x_new = lax.ppermute(x_new, 'dev', steps_seen)]
    ppermute x3, starting transfers between devices: 21.2 us -> 13.6 us  [with_halo(): before = lax.ppermute(last, axis, up)]
  transfers between devices with their start and end apart: 10 -> 25, of which waited for: 6 -> 14; matrix products, arithmetic and copies ran while one was open for 1% -> 1% of each run, Pallas kernels for 0% -> 0%
where the time goes in v1:
time: 519 us; the launch traced here: 509 us
  waiting for transfers between devices  345 us (66%)
  starting transfers between devices  51.5 us (10%)
  local copies, waits for them, and re-layouts  44 us (8%)
  matrix products  26.3 us (5%)
  other arithmetic  15.8 us (3%)
  between operations  14.5 us (3%)
  loops' own time  12.2 us (2%)
    unnamed x4, waiting for transfers between devices  319 us
    ppermute x7, starting transfers between devices, shards(): row_out = lax.ppermute(row_out, 'dev', copies)  31.4 us
    ppermute x8, waiting for transfers between devices, shards(): x_new = lax.ppermute(x_new, 'dev', steps_seen)  16.3 us
    ppermute x3, starting transfers between devices, with_halo(): before = lax.ppermute(last, axis, up)  13.6 us
    another operation x7, loops' own time, when_true(): return lax.cond(flag, compute, skipped)  12.2 us
    another operation x13, local copies, waits for them, and re-layouts  11.9 us
  transfers between devices with their start and end apart: 25, of which 14 were waited for; matrix products, arithmetic and copies ran while one was open for 1% of the time, Pallas kernels for 0%

profile of v1, /device:TPU:0, one launch (start us, length us, event | category | flops | bytes accessed | tf_op | source)
XLA Modules:
  0.0 509.0 jit_solution(7866734774150191041)
XLA Ops:
  6.5 40.0 %conditional.8 = (bf16[5,1408]{1,0:T(8,128)(2,1)S(1)}, bf16[320,1408]{1,0:T(8,128)(2,1)}) conditional(s32[]{:T(128)} %convert_element_type.90, () %tuple.65, (bf16[5,64,1408]{2,1,0:T(8,128)(2,1)}, f32[1,1408]{1,0:T(1,128)}, bf16[1408,4224]{1,0:T(8,128)(2,1)}, bf16[1408,1408]{1,0:T(8,128)(2,1)}) %tuple.148), branch_computations={%region_0.0_spmd, %region_1.0_spmd} | conditional | flops 5198732288 | bytes 54580020 | solution.py:42
  10.3 9.1 %convolution_convert_fusion.1 = bf16[320,4224]{1,0:T(8,128)(2,1)S(1)} fusion(bf16[320,1408]{1,0:T(8,128)(2,1)S(1)} %fusion.44, bf16[1408,4224]{1,0:T(8,128)(2,1)} %get-tuple-element.100), kind=kOutput, calls=%fused_computation.55 | convolution fusion | flops 3807682560 | bytes 15499264 | tf_op jit(solution)/shard_map/cond/branch_1_fun/dot_general | solution.py:99
  19.4 8.5 %reshape.116 = bf16[5,64,3,16,88]{4,3,2,1,0:T(8,128)(2,1)} reshape(bf16[320,4224]{1,0:T(8,128)(2,1)S(1)} %convolution_convert_fusion.1) | data formatting | bytes 5406720 | tf_op jit(solution)/shard_map/cond/branch_1_fun/reshape | solution.py:100
  39.6 5.3 %convolution_add_fusion = f32[320,1408]{1,0:T(8,128)} fusion(bf16[320,1408]{1,0:T(8,128)(2,1)} %reshape.117, bf16[1408,1408]{1,0:T(8,128)(2,1)} %get-tuple-element.101, bf16[320,1408]{1,0:T(8,128)(2,1)S(1)} %bitcast.143), kind=kOutput, calls=%fused_computation.56 | convolution fusion | flops 1269678080 | bytes 7569408 | tf_op jit(solution)/shard_map/cond/branch_1_fun/dot_general | solution.py:115
  49.3 4.9 collective-permute-start.2
  55.7 4.4 collective-permute-start.4
  61.6 4.4 collective-permute-start.6
  67.5 4.4 collective-permute-start.8
  73.5 4.4 collective-permute-start.10
  79.4 4.4 collective-permute-start.12
  85.3 4.4 collective-permute-start.14
  91.2 5.9 %collective-permute-done.15 = bf16[5,1408]{1,0:T(8,128)(2,1)S(1)} collective-permute-done((bf16[5,1408]{1,0:T(8,128)(2,1)S(1)}, bf16[5,1408]{1,0:T(8,128)(2,1)S(1)}, u32[]{:S(2)}, u32[]{:S(2)}) %collective-permute-start.15) | collective-permute-done | bytes 14112 | tf_op jit(solution)/shard_map/ppermute | solution.py:136
  97.2 4.4 conditional.9
  118.7 6.1 %conditional.10 = (f32[3,16,128,384]{3,2,1,0:T(8,128)}, f32[3,16,128]{2,1,0:T(8,128)S(1)}, bf16[384,1408]{0,1:T(8,128)(2,1)}) conditional(s32[]{:T(128)} %convert_element_type.91, () %tuple.63, (pred[3,384]{1,0:T(4,128)(4,1)S(1)}, bf16[3,128,16,88]{1,0,3,2:T(4,128)(2,1)}, bf16[3,384,16,88]{1,3,2,0:T(8,128)(2,1)S(1)}, ...), branch_computations={%region_9.10_spmd, %region_10.13_spmd} | conditional | flops 856958976 | bytes 60534224 | solution.py:42
  118.7 4.8 broadcast.169
  124.8 6.0 %conditional.11 = (f32[3,16,128]{2,0,1:T(4,128)S(1)}, bf16[384,1408]{0,1:T(8,128)(2,1)}, bf16[384,1408]{0,1:T(8,128)(2,1)}) conditional(s32[]{:T(128)} %convert_element_type.91, () %tuple.72, (bf16[384,1408]{1,0:T(8,128)(2,1)}, bf16[1408,1408]{1,0:T(8,128)(2,1)}, bf16[384,1408]{0,1:T(8,128)(2,1)}, bf16[3,384,16,88]{1,3,2,0:T(8,128)(2,1)}, ...), branch_computations={%region_13.14_spmd, %region_14.16_spmd} | conditional | flops 2363320320 | bytes 39649360 | solution.py:42
  134.7 6.4 %collective-permute-start.18 = (bf16[128,2816]{0,1:T(8,128)(2,1)S(1)}, bf16[128,2816]{0,1:T(8,128)(2,1)S(1)}, u32[]{:S(2)}, u32[]{:S(2)}) collective-permute-start(bf16[128,2816]{0,1:T(8,128)(2,1)S(1)} %get-tuple-element.626), channel_id=1, source_target_pairs={{0,1},{1,2},{2,3},{3,4},{4,5},{5,6},{6,7},{7,8},{8,9},{9,10},{10,1... | collective-permute-start | bytes 2162696 | tf_op jit(solution)/shard_map/ppermute | solution.py:26
  142.4 5.0 collective-permute-start.20
  155.0 8.4 %conditional.13 = (f32[80,1408]{1,0:T(8,128)}) conditional(s32[]{:T(128)} %convert_element_type.91, () %tuple.71, (f32[384,1]{0,1:T(1,128)S(1)}, bf16[384,1408]{0,1:T(8,128)(2,1)}, bf16[384,2816]{0,1:T(8,128)(2,1)S(1)}, bf16[1408,4224]{1,0:T(8,128)(2,1)}, f32[1,1408]{1,0:T(1,128)}, /*index=5*/f32[384,1408]{1,0:T(8,128)}, ...), branch_computations={%region_18.19_spmd, %region_19.21_spmd} | conditional | flops 5097455616 | bytes 36246600 | solution.py:42
  164.8 215.3 %all-reduce.4.cloned.1.call-done = f32[80,1408]{1,0:T(8,128)} async-done(((f32[80,1408]{1,0:T(8,128)}), f32[80,1408]{1,0:T(8,128)}) %all-reduce.4.cloned.1.call-update) | async-done | bytes 450576
  382.2 4.7 collective-permute-done.22
  388.4 10.3 %conditional.15 = (f32[1408,1408]{1,0:T(8,128)}) conditional(s32[]{:T(128)} %convert_element_type.90, (bf16[384,1408]{0,1:T(8,128)(2,1)}, bf16[384,1408]{1,0:T(8,128)(2,1)S(1)}) %tuple.142, (bf16[320,1408]{1,0:T(8,128)(2,1)}, f32[320,1408]{1,0:T(8,128)S(1)}) %tuple.78), branch_computations={%region_24.25_spmd, %region_25.26_spmd} | conditional | flops 7612661760 | bytes 10633224 | solution.py:295
  388.4 10.3 %fusion.83 = f32[1408,1408]{1,0:T(8,128)} fusion(bf16[320,1408]{1,0:T(8,128)(2,1)} %get-tuple-element.136, f32[320,1408]{1,0:T(8,128)S(1)} %get-tuple-element.137), kind=kOutput, calls=%fused_computation.129 | convolution fusion | flops 7612661760 | bytes 10633216 | tf_op jit(solution)/shard_map/cond/branch_1_fun/dot_general | solution.py:52
  398.7 103.3 %reduce-scatter.4.cloned.1.call-done = f32[88,1408]{1,0:T(8,128)} async-done(((f32[1408,1408]{1,0:T(8,128)}), f32[88,1408]{1,0:T(8,128)}) %reduce-scatter.4.cloned.1.call-update) | async-done | bytes 495632
  (104 shorter events, 74.3 us)
Async XLA Ops:
  6.5 373.5 %all-reduce.4.cloned.1.call-start = ((), (), s32[]{:S(2)}) async-start(), calls=%async_computation.1 | async-start | bytes 901120
  49.3 6.4 %collective-permute-start.1 = (bf16[5,1408]{1,0:T(8,128)(2,1)S(1)}, bf16[5,1408]{1,0:T(8,128)(2,1)S(1)}, u32[]{:S(2)}, u32[]{:S(2)}) collective-permute-start(bf16[5,1408]{1,0:T(8,128)(2,1)S(1)} %collective-permute-done), channel_id=1, source_target_pairs={{0,1},{1,2},{2,3},{3,4},{4,5},{5,6},{6,7},{7,8},{8,9},{9,10},{10,1... | collective-permute-start | bytes 42248 | tf_op jit(solution)/shard_map/ppermute | solution.py:136
  49.3 6.4 %collective-permute-start.2 = (bf16[5,1408]{1,0:T(8,128)(2,1)S(1)}, bf16[5,1408]{1,0:T(8,128)(2,1)S(1)}, u32[]{:S(2)}, u32[]{:S(2)}) collective-permute-start(bf16[5,1408]{1,0:T(8,128)(2,1)S(1)} %collective-permute-done), channel_id=1, source_target_pairs={{0,15},{1,0},{2,1},{3,2},{4,3},{5,4},{6,5},{7,6},{8,7},{9,8},{10,9... | collective-permute-start | bytes 42248 | tf_op jit(solution)/shard_map/ppermute | solution.py:146
  55.7 5.9 %collective-permute-start.3 = (bf16[5,1408]{1,0:T(8,128)(2,1)S(1)}, bf16[5,1408]{1,0:T(8,128)(2,1)S(1)}, u32[]{:S(2)}, u32[]{:S(2)}) collective-permute-start(bf16[5,1408]{1,0:T(8,128)(2,1)S(1)} %collective-permute-done.1), channel_id=1, source_target_pairs={{0,1},{1,2},{2,3},{3,4},{4,5},{5,6},{6,7},{7,8},{8,9},{9,10},{10,1... | collective-permute-start | bytes 42248 | tf_op jit(solution)/shard_map/ppermute | solution.py:136
  55.7 5.9 %collective-permute-start.4 = (bf16[5,1408]{1,0:T(8,128)(2,1)S(1)}, bf16[5,1408]{1,0:T(8,128)(2,1)S(1)}, u32[]{:S(2)}, u32[]{:S(2)}) collective-permute-start(bf16[5,1408]{1,0:T(8,128)(2,1)S(1)} %collective-permute-done.2), channel_id=1, source_target_pairs={{0,15},{1,0},{2,1},{3,2},{4,3},{5,4},{6,5},{7,6},{8,7},{9,8},{10,9... | collective-permute-start | bytes 42248 | tf_op jit(solution)/shard_map/ppermute | solution.py:146
  61.6 5.9 %collective-permute-start.5 = (bf16[5,1408]{1,0:T(8,128)(2,1)S(1)}, bf16[5,1408]{1,0:T(8,128)(2,1)S(1)}, u32[]{:S(2)}, u32[]{:S(2)}) collective-permute-start(bf16[5,1408]{1,0:T(8,128)(2,1)S(1)} %collective-permute-done.3), channel_id=1, source_target_pairs={{0,1},{1,2},{2,3},{3,4},{4,5},{5,6},{6,7},{7,8},{8,9},{9,10},{10,1... | collective-permute-start | bytes 42248 | tf_op jit(solution)/shard_map/ppermute | solution.py:136
  61.6 5.9 %collective-permute-start.6 = (bf16[5,1408]{1,0:T(8,128)(2,1)S(1)}, bf16[5,1408]{1,0:T(8,128)(2,1)S(1)}, u32[]{:S(2)}, u32[]{:S(2)}) collective-permute-start(bf16[5,1408]{1,0:T(8,128)(2,1)S(1)} %collective-permute-done.4), channel_id=1, source_target_pairs={{0,15},{1,0},{2,1},{3,2},{4,3},{5,4},{6,5},{7,6},{8,7},{9,8},{10,9... | collective-permute-start | bytes 42248 | tf_op jit(solution)/shard_map/ppermute | solution.py:146
  67.5 5.9 %collective-permute-start.7 = (bf16[5,1408]{1,0:T(8,128)(2,1)S(1)}, bf16[5,1408]{1,0:T(8,128)(2,1)S(1)}, u32[]{:S(2)}, u32[]{:S(2)}) collective-permute-start(bf16[5,1408]{1,0:T(8,128)(2,1)S(1)} %collective-permute-done.5), channel_id=1, source_target_pairs={{0,1},{1,2},{2,3},{3,4},{4,5},{5,6},{6,7},{7,8},{8,9},{9,10},{10,1... | collective-permute-start | bytes 42248 | tf_op jit(solution)/shard_map/ppermute | solution.py:136
  67.5 5.9 %collective-permute-start.8 = (bf16[5,1408]{1,0:T(8,128)(2,1)S(1)}, bf16[5,1408]{1,0:T(8,128)(2,1)S(1)}, u32[]{:S(2)}, u32[]{:S(2)}) collective-permute-start(bf16[5,1408]{1,0:T(8,128)(2,1)S(1)} %collective-permute-done.6), channel_id=1, source_target_pairs={{0,15},{1,0},{2,1},{3,2},{4,3},{5,4},{6,5},{7,6},{8,7},{9,8},{10,9... | collective-permute-start | bytes 42248 | tf_op jit(solution)/shard_map/ppermute | solution.py:146
  73.4 5.9 %collective-permute-start.9 = (bf16[5,1408]{1,0:T(8,128)(2,1)S(1)}, bf16[5,1408]{1,0:T(8,128)(2,1)S(1)}, u32[]{:S(2)}, u32[]{:S(2)}) collective-permute-start(bf16[5,1408]{1,0:T(8,128)(2,1)S(1)} %collective-permute-done.7), channel_id=1, source_target_pairs={{0,1},{1,2},{2,3},{3,4},{4,5},{5,6},{6,7},{7,8},{8,9},{9,10},{10,1... | collective-permute-start | bytes 42248 | tf_op jit(solution)/shard_map/ppermute | solution.py:136
  73.5 5.9 %collective-permute-start.10 = (bf16[5,1408]{1,0:T(8,128)(2,1)S(1)}, bf16[5,1408]{1,0:T(8,128)(2,1)S(1)}, u32[]{:S(2)}, u32[]{:S(2)}) collective-permute-start(bf16[5,1408]{1,0:T(8,128)(2,1)S(1)} %collective-permute-done.8), channel_id=1, source_target_pairs={{0,15},{1,0},{2,1},{3,2},{4,3},{5,4},{6,5},{7,6},{8,7},{9,8},{10,9... | collective-permute-start | bytes 42248 | tf_op jit(solution)/shard_map/ppermute | solution.py:146
  79.4 5.9 %collective-permute-start.11 = (bf16[5,1408]{1,0:T(8,128)(2,1)S(1)}, bf16[5,1408]{1,0:T(8,128)(2,1)S(1)}, u32[]{:S(2)}, u32[]{:S(2)}) collective-permute-start(bf16[5,1408]{1,0:T(8,128)(2,1)S(1)} %collective-permute-done.9), channel_id=1, source_target_pairs={{0,1},{1,2},{2,3},{3,4},{4,5},{5,6},{6,7},{7,8},{8,9},{9,10},{10,1... | collective-permute-start | bytes 42248 | tf_op jit(solution)/shard_map/ppermute | solution.py:136
  79.4 5.9 %collective-permute-start.12 = (bf16[5,1408]{1,0:T(8,128)(2,1)S(1)}, bf16[5,1408]{1,0:T(8,128)(2,1)S(1)}, u32[]{:S(2)}, u32[]{:S(2)}) collective-permute-start(bf16[5,1408]{1,0:T(8,128)(2,1)S(1)} %collective-permute-done.10), channel_id=1, source_target_pairs={{0,15},{1,0},{2,1},{3,2},{4,3},{5,4},{6,5},{7,6},{8,7},{9,8},{10,9... | collective-permute-start | bytes 42248 | tf_op jit(solution)/shard_map/ppermute | solution.py:146
  85.3 5.9 %collective-permute-start.13 = (bf16[5,1408]{1,0:T(8,128)(2,1)S(1)}, bf16[5,1408]{1,0:T(8,128)(2,1)S(1)}, u32[]{:S(2)}, u32[]{:S(2)}) collective-permute-start(bf16[5,1408]{1,0:T(8,128)(2,1)S(1)} %collective-permute-done.11), channel_id=1, source_target_pairs={{0,1},{1,2},{2,3},{3,4},{4,5},{5,6},{6,7},{7,8},{8,9},{9,10},{10,1... | collective-permute-start | bytes 42248 | tf_op jit(solution)/shard_map/ppermute | solution.py:136
  85.3 5.9 %collective-permute-start.14 = (bf16[5,1408]{1,0:T(8,128)(2,1)S(1)}, bf16[5,1408]{1,0:T(8,128)(2,1)S(1)}, u32[]{:S(2)}, u32[]{:S(2)}) collective-permute-start(bf16[5,1408]{1,0:T(8,128)(2,1)S(1)} %collective-permute-done.12), channel_id=1, source_target_pairs={{0,15},{1,0},{2,1},{3,2},{4,3},{5,4},{6,5},{7,6},{8,7},{9,8},{10,9... | collective-permute-start | bytes 42248 | tf_op jit(solution)/shard_map/ppermute | solution.py:146
  91.2 5.9 %collective-permute-start.15 = (bf16[5,1408]{1,0:T(8,128)(2,1)S(1)}, bf16[5,1408]{1,0:T(8,128)(2,1)S(1)}, u32[]{:S(2)}, u32[]{:S(2)}) collective-permute-start(bf16[5,1408]{1,0:T(8,128)(2,1)S(1)} %collective-permute-done.13), channel_id=1, source_target_pairs={{0,1},{1,2},{2,3},{3,4},{4,5},{5,6},{6,7},{7,8},{8,9},{9,10},{10,1... | collective-permute-start | bytes 42248 | tf_op jit(solution)/shard_map/ppermute | solution.py:136
  106.8 5.9 %collective-permute-start.16 = (bf16[128,2816]{0,1:T(8,128)(2,1)}, bf16[128,2816]{0,1:T(8,128)(2,1)}, u32[]{:S(2)}, u32[]{:S(2)}) collective-permute-start(bf16[128,2816]{0,1:T(8,128)(2,1)} %get-tuple-element.630), channel_id=1, source_target_pairs={{0,1},{1,2},{2,3},{3,4},{4,5},{5,6},{6,7},{7,8},{8,9},{9,10},{10,1... | collective-permute-start | bytes 2162696 | tf_op jit(solution)/shard_map/ppermute | solution.py:26
  109.0 4.2 collective-permute-start.17
  134.7 17.1 %collective-permute-start.18 = (bf16[128,2816]{0,1:T(8,128)(2,1)S(1)}, bf16[128,2816]{0,1:T(8,128)(2,1)S(1)}, u32[]{:S(2)}, u32[]{:S(2)}) collective-permute-start(bf16[128,2816]{0,1:T(8,128)(2,1)S(1)} %get-tuple-element.626), channel_id=1, source_target_pairs={{0,1},{1,2},{2,3},{3,4},{4,5},{5,6},{6,7},{7,8},{8,9},{9,10},{10,1... | collective-permute-start | bytes 2162696 | tf_op jit(solution)/shard_map/ppermute | solution.py:26
  141.1 10.7 %collective-permute-start.19 = (bf16[128,2816]{0,1:T(8,128)(2,1)S(1)}, bf16[128,2816]{0,1:T(8,128)(2,1)S(1)}, u32[]{:S(2)}, u32[]{:S(2)}) collective-permute-start(bf16[128,2816]{0,1:T(8,128)(2,1)S(1)} %get-tuple-element.627), channel_id=1, source_target_pairs={{1,0},{2,1},{3,2},{4,3},{5,4},{6,5},{7,6},{8,7},{9,8},{10,9},{11,1... | collective-permute-start | bytes 2162696 | tf_op jit(solution)/shard_map/ppermute | solution.py:27
  142.4 6.3 %collective-permute-start.20 = (f32[128,32]{0,1:T(8,128)S(1)}, f32[128,32]{0,1:T(8,128)S(1)}, u32[]{:S(2)}, u32[]{:S(2)}) collective-permute-start(f32[128,32]{0,1:T(8,128)S(1)} %get-tuple-element.632), channel_id=1, source_target_pairs={{0,1},{1,2},{2,3},{3,4},{4,5},{5,6},{6,7},{7,8},{8,9},{9,10},{10,1... | collective-permute-start | bytes 49160 | tf_op jit(solution)/shard_map/ppermute | solution.py:26
  147.4 4.3 collective-permute-start.21
  163.5 338.5 %reduce-scatter.4.cloned.1.call-start = ((), (), s32[]{:S(2)}) async-start(), calls=%async_computation.2 | async-start | bytes 8425472
  380.9 6.0 %collective-permute-start.22 = (f32[5,1408]{1,0:T(8,128)S(1)}, f32[5,1408]{1,0:T(8,128)S(1)}, u32[]{:S(2)}, u32[]{:S(2)}) collective-permute-start(f32[5,1408]{1,0:T(8,128)S(1)} %constant_dynamic-slice_fusion), channel_id=1, source_target_pairs={{16,0},{17,1},{18,2},{19,3},{20,4},{21,5},{22,6},{23,7},{24,8},{25... | collective-permute-start | bytes 84488 | tf_op jit(solution)/shard_map/ppermute | solution.py:16
  (10 other events, 221.5 us)
Sparse Core Ops, SparseCore 0:
  163.6 216.4 all-reduce.3
  398.8 103.0 reduce-scatter.3
